TPU v7x, 32 devices: a whole 2x2x4 slice. The times are simulated.
32 devices in a mesh: samp: 16 (over z, y, x), pos: 2 (over core).
Axes of the slice: x: 2, y: 2, z: 4, core: 2. Of those that a mesh axis runs over, the one named last changes fastest.
Arguments:
- dosages: bfloat16 [32768, 4096], P('samp', 'pos')
- phenotypes: bfloat16 [32768, 2048], P('samp')
- gene_weights: bfloat16 [4096, 16], P('pos'), may hold values from -0.1875 to 0.1875
- gene_start: int32 [16], replicated, may hold values from 0 to 3072, as said below
- gene_end: int32 [16], replicated, may hold values from 1024 to 4096, as said below
Outputs:
- variant_z: float32 [2048, 4096], P('samp', 'pos')
- gene_z: float32 [2048, 16], P('samp', 'pos')
Inputs may be any that keep to these rules, and one draw needn't show every extreme that they name: gene_end - gene_start lies between 1024 and 2048; some window starts at 0 and some ends at 4096. gene_end is greater than gene_start of the same gene.
All inputs are finite; a program needn't handle non-finite values.
Results may differ from a plain program's by a relative error of at most 0.0029.
Values sent between devices are 32-bit elements; how exact they have to be, the bound alone decides.
A program may use at most 128 MiB of HBM per device.

v0:
```python
import jax
import jax.numpy as jnp
from jax import lax
from jax.sharding import PartitionSpec as P

EPSILON = 1e-06


def contract(left, right):
    return lax.dot_general(
        left, right, (((0,), (0,)), ((), ())), preferred_element_type=jnp.float32
    )


def per_device(dosages, phenotypes, gene_weights, gene_start, gene_end):
    width_here = dosages.shape[1]
    gene_count = gene_weights.shape[1]
    gene_share = gene_count // lax.axis_size("pos")
    offset = lax.axis_index("pos") * width_here
    position = offset + lax.broadcasted_iota(jnp.int32, (width_here, gene_count), 0)
    inside = (position >= gene_start[None, :]) & (position < gene_end[None, :])
    masked = jnp.where(inside, gene_weights, jnp.zeros_like(gene_weights))
    partial_value = jnp.dot(dosages, masked, preferred_element_type=jnp.float32)
    summed = lax.psum(partial_value, "pos")
    predicted = lax.dynamic_slice_in_dim(summed, lax.axis_index("pos") * gene_share, gene_share, 1)
    pred_low = predicted.astype(jnp.bfloat16)
    samples = dosages.shape[0] * lax.axis_size("samp")
    dose_sq = jnp.sum(jnp.square(dosages.astype(jnp.float32)), axis=0)
    pred_sq = jnp.sum(predicted * predicted, axis=0)
    trait_sq = jnp.sum(jnp.square(phenotypes.astype(jnp.float32)), axis=0)
    joined = lax.psum_scatter(
        jnp.concatenate(
            [contract(phenotypes, dosages), contract(phenotypes, pred_low), trait_sq[:, None]],
            axis=1,
        ),
        "samp",
        scatter_dimension=0,
        tiled=True,
    )
    marginal = joined[:, :width_here]
    gene_cross = joined[:, width_here : width_here + gene_share]
    trait_own = joined[:, width_here + gene_share]
    dose_total, pred_total = lax.psum((dose_sq, pred_sq), "samp")
    mean_dose = dose_total / samples
    mean_pred = pred_total / samples
    mean_trait = trait_own / samples
    variant_z = marginal / jnp.sqrt(
        samples * (mean_trait[:, None] + EPSILON) * (mean_dose[None, :] + EPSILON)
    )
    gene_z = gene_cross / jnp.sqrt(
        samples * (mean_trait[:, None] + EPSILON) * (mean_pred[None, :] + EPSILON)
    )
    return (variant_z, gene_z)


def solution(mesh):
    return jax.shard_map(
        per_device,
        mesh=mesh,
        in_specs=(P("samp", "pos"), P("samp", None), P("pos", None), P(), P()),
        out_specs=(P("samp", "pos"), P("samp", "pos")),
        check_vma=False,
    )
```

profile of v0, /device:TPU:0, one launch (start us, length us, event | category | flops | bytes accessed | tf_op | source)
XLA Modules:
  0.0 338.5 jit_solution(8167828639336624725)
XLA Ops:
  7.2 0.0 all-reduce.3.cloned.1.call-start
  7.2 6.4 %convolution_bitcast_fusion = f32[2048,16]{0,1:T(8,128)} fusion(bf16[2048,2048]{1,0:T(8,128)(2,1)} %param.5, bf16[2048,16]{0,1:T(8,128)(2,1)} %param.7, s32[2048]{0:T(1024)S(1)} %iota_add_fusion, s32[16]{0:T(128)} %param.9, s32[16]{0:T(128)} %param.8), kind=kOutput, calls=%fused_computation.3 | convolution fusion | flops 134348800 | bytes 8593536 | tf_op jit(solution)/shard_map/dot_general | solution.py:23
  13.6 0.0 all-reduce.3.cloned.1.call-update
  13.6 0.0 reduce-scatter.2.cloned.1.call-start
  13.7 24.4 %fusion.9 = f32[2048,2048]{0,1:T(8,128)} fusion(bf16[2048,2048]{1,0:T(8,128)(2,1)} %param.6, bf16[2048,2048]{1,0:T(8,128)(2,1)} %param.5), kind=kOutput, calls=%fused_computation.23 | convolution fusion | flops 17179869184 | bytes 33554432 | tf_op jit(solution)/shard_map/dot_general | solution.py:10
  38.1 5.1 %multiply_reduce_fusion.1 = f32[2048]{0:T(1024)S(1)} fusion(bf16[2048,2048]{1,0:T(8,128)(2,1)} %param.6), kind=kLoop, calls=%fused_computation.2 | loop fusion | flops 12580864 | bytes 8396800 | tf_op jit(solution)/shard_map/reduce_sum | solution.py:30
  43.2 0.0 all-reduce.3.cloned.1.call-done
  43.2 4.6 %convolution_bitcast_fusion.1 = f32[2048,8]{0,1:T(8,128)S(1)} fusion(bf16[2048,2048]{1,0:T(8,128)(2,1)} %param.6, f32[2048,16]{0,1:T(8,128)} %all-reduce.3.cloned.1.call-done, s32[]{:T(128)S(6)} %select_n.8), kind=kOutput, calls=%fused_computation.4 | convolution fusion | flops 67108864 | bytes 8486916 | tf_op jit(solution)/shard_map/dot_general | solution.py:10
  47.8 11.6 %pad_maximum_fusion = f32[2048,2057]{0,1:T(8,128)} fusion(f32[2048,1]{0,1:T(1,128)S(1)} %bitcast.11, f32[2048,8]{0,1:T(8,128)S(1)} %convolution_bitcast_fusion.1, f32[2048,2048]{0,1:T(8,128)} %fusion.9), kind=kLoop, calls=%fused_computation | loop fusion | flops 8425472 | bytes 33701888 | tf_op jit(solution)/shard_map/concatenate | solution.py:32
  59.5 0.0 reduce-scatter.2.cloned.1.call-update
  59.5 0.0 copy-start
  59.5 5.1 %multiply_reduce_fusion = f32[2048]{0:T(1024)S(1)} fusion(bf16[2048,2048]{1,0:T(8,128)(2,1)} %param.5), kind=kLoop, calls=%fused_computation.1 | loop fusion | flops 12580864 | bytes 8396800 | tf_op jit(solution)/shard_map/reduce_sum | solution.py:28
  64.7 0.0 copy-done
  64.7 0.1 multiply_reduce_fusion.2
  64.8 48.0 %all-reduce = (f32[2048]{0:T(1024)S(1)}, f32[8]{0:T(128)S(1)}) all-reduce(f32[2048]{0:T(1024)S(1)} %multiply_reduce_fusion, f32[8]{0:T(128)S(1)} %multiply_reduce_fusion.2), channel_id=1, replica_groups=mesh['samp'=16,'pos'=2] {'samp'}, use_global_device_ids=true, to_apply=%region_4.5 | all-reduce | flops 2056 | bytes 16448 | tf_op jit(solution)/shard_map/psum | solution.py:43
  112.8 213.9 %reduce-scatter.2.cloned.1.call-done = f32[128,2057]{0,1:T(8,128)} async-done(((f32[2048,2057]{0,1:T(8,128)}), f32[128,2057]{0,1:T(8,128)}) %reduce-scatter.2.cloned.1.call-update) | async-done | bytes 1053200 | tf_op jit(solution)/shard_map/reduce_scatter | solution.py:31
  326.7 0.7 fusion.6
  327.4 1.6 slice_multiply_fusion
  329.0 1.3 copy.7
  330.3 1.4 slice_multiply_fusion.1
  (3 shorter events, 0.0 us)
Async XLA Ops:
  7.2 36.1 %all-reduce.3.cloned.1.call-start = ((), (), s32[]{:S(2)}) async-start(), calls=%async_computation.1 | async-start | bytes 262144 | tf_op jit(solution)/shard_map/psum | solution.py:24
  13.6 313.1 %reduce-scatter.2.cloned.1.call-start = ((), (), s32[]{:S(2)}) async-start(), calls=%async_computation.2 | async-start | bytes 17965056 | tf_op jit(solution)/shard_map/reduce_scatter | solution.py:31
  59.5 5.2 %copy-start = (f32[2048,16]{0,1:T(8,128)S(1)}, f32[2048,16]{0,1:T(8,128)}, u32[]{:S(2)}) copy-start(f32[2048,16]{0,1:T(8,128)} %all-reduce.3.cloned.1.call-done) | copy-start | bytes 393220
Sparse Core Ops, SparseCore 0:
  13.8 20.6 all-reduce.2
  59.6 267.0 reduce-scatter.1
where the time goes:
time: 339 us; the launch traced here: 338 us
  waiting for transfers between devices  214 us (63%)
  blocking collectives  48 us (14%)
  matrix products  35.4 us (10%)
  other arithmetic  25.7 us (8%)
  between operations  14.1 us (4%)
    reduce_scatter x1, waiting for transfers between devices, per_device(): lax.psum_scatter(jnp.concatenate([contract(phenotypes, dosages), contract...  214 us
    psum x1, blocking collectives, per_device(): dose_total, pred_total = lax.psum((dose_sq, pred_sq), 'samp')  48 us
    dot_general x2, matrix products, contract(): lax.dot_general(left, right, (((0,), (0,)), ((), ())), preferred_element_...  29 us
    concatenate x1, other arithmetic, per_device(): jnp.concatenate([contract(phenotypes, dosages), contract(phenotypes, pred...  11.6 us
  transfers between devices with their start and end apart: 2, of which 1 were waited for; matrix products, arithmetic and copies ran while one was open for 10% of the time, Pallas kernels for 0%

commit v1 on v0

v1 whole, which is shorter than its diff:
```python
import functools

import jax
import jax.numpy as jnp
from jax import lax
from jax.experimental import pallas as pl
from jax.experimental.pallas import tpu as pltpu
from jax.sharding import PartitionSpec as P

EPSILON = 1e-06
WIDTH = 128
MESH = pl.DeviceIdType.MESH


def kernel(
    nz, npos, share, dos, ph, wt, out, ex_out, ar_out,
    part, r1, r2, r3, xt, ex, e1, e2, e3, ar, a1, a2, a3, pp, pr, pf,
    s_sem, v_sem, s3_sem, v3_sem, es_sem, ev_sem, es3_sem, ev3_sem, ps_sem, pv_sem,
):
    samples, variants = dos.shape
    traits = ph.shape[1]
    chunks, w, block = part.shape[0], part.shape[4], part.shape[5]
    tile = 2 * block
    me = lax.axis_index("samp")
    mp = lax.axis_index("pos")
    mx = lax.rem(me, 2)
    my = lax.rem(me // 2, 2)
    mz = me // 4
    xp = (mz * 4 + my * 2 + (1 - mx), mp)
    yp = (mz * 4 + (1 - my) * 2 + mx, mp)

    def zpeer(d):
        return lax.rem(mz + d, nz)

    def zdev(d):
        return (zpeer(d) * 4 + my * 2 + mx, mp)

    def ppeer(d):
        return lax.rem(mp + d, npos)

    barrier = pltpu.get_barrier_semaphore()
    peers = [xp, yp] + [zdev(d) for d in range(1, nz)]
    peers += [(me, ppeer(d)) for d in range(1, npos)]
    for peer in peers:
        pl.semaphore_signal(barrier, inc=1, device_id=peer, device_id_type=MESH)
    pl.semaphore_wait(barrier, len(peers))

    def remote(src, dst, send, recv, dev):
        return pltpu.make_async_remote_copy(
            src_ref=src, dst_ref=dst, send_sem=send, recv_sem=recv,
            device_id=dev, device_id_type=MESH,
        )

    def order(c):
        return (mx, my, xp, yp) if c % 2 == 0 else (my, mx, yp, xp)

    def compute(c):
        cols = slice(c * w, (c + 1) * w)
        xt[...] = dos[:, cols].T

        def body(i, carry):
            res = jnp.dot(
                xt[...],
                ph[:, pl.ds(pl.multiple_of(i * tile, tile), tile)],
                preferred_element_type=jnp.float32,
            )
            z, y = i // 2, lax.rem(i, 2)
            for x in range(2):
                val = res[:, x * block : (x + 1) * block]
                if c % 2 == 0:
                    part[c, x, y, z] = val
                else:
                    part[c, y, x, z] = val
            return carry

        lax.fori_loop(0, 2 * nz, body, 0)

    def copy1(c):
        f, _, dev, _ = order(c)
        return remote(part.at[c, 1 - f], r1.at[c], s_sem.at[0, c], v_sem.at[0, c], dev)

    def copy2(c):
        f, s, _, dev = order(c)
        return remote(part.at[c, f, 1 - s], r2.at[c], s_sem.at[1, c], v_sem.at[1, c], dev)

    def copy3(c, d):
        f, s, _, _ = order(c)
        return remote(
            part.at[c, f, s, zpeer(d)], r3.at[c, d - 1],
            s3_sem.at[c, d - 1], v3_sem.at[c, d - 1], zdev(d),
        )

    def add1(c, other):
        f, s, _, _ = order(c)
        k = 1 - s if other else s

        def body(z, carry):
            part[c, f, k, z] = part[c, f, k, z] + r1[c, k, z]
            return carry

        lax.fori_loop(0, nz, body, 0)

    def stage2(c):
        copy1(c).wait_recv()
        add1(c, True)
        copy2(c).start()
        add1(c, False)

    def stage3(c):
        f, s, _, _ = order(c)
        copy2(c).wait_recv()

        def body(z, carry):
            part[c, f, s, z] = part[c, f, s, z] + r2[c, z]
            return carry

        lax.fori_loop(0, nz, body, 0)
        for d in range(nz - 1, 0, -1):
            copy3(c, d).start()

    def finish(c):
        f, s, _, _ = order(c)
        total = part[c, f, s, mz]
        for d in range(1, nz):
            copy3(c, d).wait_recv()
            total = total + r3[c, d - 1]
        out[c] = total

    def pcopy(d):
        return remote(
            pp.at[ppeer(d)], pr.at[d - 1], ps_sem.at[d - 1], pv_sem.at[d - 1],
            (me, ppeer(d)),
        )

    def predict():
        step = min(samples, 256)

        def body(i, carry):
            rows = pl.ds(pl.multiple_of(i * step, step), step)
            res = lax.dot_general(
                wt[...], dos[rows, :], (((1,), (1,)), ((), ())),
                preferred_element_type=jnp.float32,
            )
            for q in range(npos):
                pp[q, :, rows] = res[q * share : (q + 1) * share]
            return carry

        lax.fori_loop(0, samples // step, body, 0)
        for d in range(1, npos):
            pcopy(d).start()

    def squares(ref, cols, width):
        step = min(samples, 128)

        def body(i, acc):
            v = ref[pl.ds(pl.multiple_of(i * step, step), step), cols].astype(jnp.float32)
            return acc + jnp.sum(v * v, axis=0, keepdims=True)

        return lax.fori_loop(0, samples // step, body, jnp.zeros((1, width), jnp.float32))

    def small():
        pred = pp[mp]
        for d in range(1, npos):
            pcopy(d).wait_recv()
            pred = pred + pr[d - 1]
        pf[...] = jnp.zeros_like(pf)
        pf[0:share, :] = pred
        full = pf[...]
        low = full.astype(jnp.bfloat16)
        ar[chunks : chunks + pf.shape[0], :] = jnp.broadcast_to(
            jnp.sum(full * full, axis=1, keepdims=True), (pf.shape[0], w)
        )
        for c in range(chunks):
            ar[c : c + 1, :] = squares(dos, slice(c * w, (c + 1) * w), w)
        g = pf.shape[0]

        def body(i, carry):
            cols = pl.ds(pl.multiple_of(i * tile, tile), tile)
            res = jnp.dot(low, ph[:, cols], preferred_element_type=jnp.float32)
            tsq = jnp.broadcast_to(squares(ph, cols, tile), (8, tile))
            z, y = i // 2, lax.rem(i, 2)
            for x in range(2):
                ex[x, y, z, 0:g, :] = res[:, x * block : (x + 1) * block]
                ex[x, y, z, g : g + 8, :] = tsq[:, x * block : (x + 1) * block]
            return carry

        lax.fori_loop(0, 2 * nz, body, 0)

    ecopy1 = remote(ex.at[1 - mx], e1, es_sem.at[0], ev_sem.at[0], xp)
    acopy1 = remote(ar, a1, es_sem.at[1], ev_sem.at[1], xp)
    ecopy2 = remote(ex.at[mx, 1 - my], e2, es_sem.at[2], ev_sem.at[2], yp)
    acopy2 = remote(ar_out, a2, es_sem.at[3], ev_sem.at[3], yp)

    def ecopy3(d):
        return remote(
            ex.at[mx, my, zpeer(d)], e3.at[d - 1],
            es3_sem.at[0, d - 1], ev3_sem.at[0, d - 1], zdev(d),
        )

    def acopy3(d):
        return remote(
            ar, a3.at[d - 1], es3_sem.at[1, d - 1], ev3_sem.at[1, d - 1], zdev(d)
        )

    def small1():
        ecopy1.start()
        acopy1.start()

    def small2():
        ecopy1.wait_recv()
        ex[mx] = ex[mx] + e1[...]
        ecopy2.start()
        acopy1.wait()
        ar_out[...] = ar[...] + a1[...]
        acopy2.start()

    def small3():
        ecopy2.wait_recv()
        ex[mx, my] = ex[mx, my] + e2[...]
        acopy2.wait()
        ar[...] = ar_out[...] + a2[...]
        for d in range(nz - 1, 0, -1):
            ecopy3(d).start()
            acopy3(d).start()

    def small4():
        total = ex[mx, my, mz]
        sums = ar[...]
        for d in range(1, nz):
            ecopy3(d).wait_recv()
            acopy3(d).wait_recv()
            total = total + e3[d - 1]
            sums = sums + a3[d - 1]
        ex_out[...] = total
        ar_out[...] = sums

    pairs = chunks // 2
    for t in range(pairs + 3):
        if t == 0:
            compute(0)
            copy1(0).start()
            compute(1)
            copy1(1).start()
        if t + 1 < pairs:
            for c in (2 * t + 2, 2 * t + 3):
                compute(c)
                copy1(c).start()
        if t == 0:
            predict()
        if t == 1:
            small()
            small1()
        if t == 2:
            small2()
        if t == 3:
            small3()
        if 0 <= t < pairs:
            for c in (2 * t, 2 * t + 1):
                stage2(c)
        if 0 <= t - 1 < pairs:
            for c in (2 * t - 2, 2 * t - 1):
                stage3(c)
        if 0 <= t - 2 < pairs:
            for c in (2 * t - 4, 2 * t - 3):
                finish(c)
    small4()
    for c in range(chunks):
        copy1(c).wait_send()
        copy2(c).wait_send()
        for d in range(1, nz):
            copy3(c, d).wait_send()
    ecopy1.wait_send()
    ecopy2.wait_send()
    for d in range(1, nz):
        ecopy3(d).wait_send()
        acopy3(d).wait_send()
    for d in range(1, npos):
        pcopy(d).wait_send()


def reduce_all(dosages, phenotypes, masked_t, n, npos, share):
    samples, variants = dosages.shape
    traits = phenotypes.shape[1]
    nz = n // 4
    block = traits // n
    w = WIDTH
    chunks = variants // w
    g = -(-share // 16) * 16
    f32 = jnp.float32
    vm = pltpu.VMEM
    dma = pltpu.SemaphoreType.DMA
    nq = max(npos - 1, 1)
    scratch = [
        vm((chunks, 2, 2, nz, w, block), f32),
        vm((chunks, 2, nz, w, block), f32),
        vm((chunks, nz, w, block), f32),
        vm((chunks, nz - 1, w, block), f32),
        vm((w, samples), jnp.bfloat16),
        vm((2, 2, nz, g + 8, block), f32),
        vm((2, nz, g + 8, block), f32),
        vm((nz, g + 8, block), f32),
        vm((nz - 1, g + 8, block), f32),
        vm((chunks + g, w), f32),
        vm((chunks + g, w), f32),
        vm((chunks + g, w), f32),
        vm((nz - 1, chunks + g, w), f32),
        vm((npos, share, samples), f32),
        vm((nq, share, samples), f32),
        vm((g, samples), f32),
        dma((2, chunks)), dma((2, chunks)),
        dma((chunks, nz - 1)), dma((chunks, nz - 1)),
        dma((4,)), dma((4,)),
        dma((2, nz - 1)), dma((2, nz - 1)),
        dma((nq,)), dma((nq,)),
    ]
    flops = 2 * samples * variants * traits
    return pl.pallas_call(
        functools.partial(kernel, nz, npos, share),
        out_shape=(
            jax.ShapeDtypeStruct((chunks, w, block), f32),
            jax.ShapeDtypeStruct((g + 8, block), f32),
            jax.ShapeDtypeStruct((chunks + g, w), f32),
        ),
        in_specs=[pl.BlockSpec(memory_space=pltpu.VMEM)] * 3,
        out_specs=[pl.BlockSpec(memory_space=pltpu.VMEM)] * 3,
        scratch_shapes=scratch,
        compiler_params=pltpu.CompilerParams(
            collective_id=0, has_side_effects=True, vmem_limit_bytes=60 * 1024 * 1024
        ),
        cost_estimate=pl.CostEstimate(
            flops=flops, bytes_accessed=2 * samples * (variants + traits), transcendentals=0
        ),
    )(dosages, phenotypes, masked_t)


def per_device(dosages, phenotypes, gene_weights, gene_start, gene_end):
    variants = dosages.shape[1]
    genes = gene_weights.shape[1]
    n, npos = lax.axis_size("samp"), lax.axis_size("pos")
    share = genes // npos
    offset = lax.axis_index("pos") * variants
    position = offset + lax.broadcasted_iota(jnp.int32, (genes, variants), 1)
    inside = (position >= gene_start[:, None]) & (position < gene_end[:, None])
    weights_t = gene_weights.T
    masked_t = jnp.where(inside, weights_t, jnp.zeros_like(weights_t))
    out, extra, sums = reduce_all(dosages, phenotypes, masked_t, n, npos, share)
    samples = dosages.shape[0] * n
    chunks = out.shape[0]
    g = sums.shape[0] - chunks
    mean_dose = sums[:chunks].reshape(-1) / samples
    mean_pred = sums[chunks : chunks + share, 0] / samples
    mean_trait = extra[g] / samples
    marginal = out.reshape(variants, -1).T
    variant_z = marginal / jnp.sqrt(
        samples * (mean_trait[:, None] + EPSILON) * (mean_dose[None, :] + EPSILON)
    )
    gene_z = extra[:share].T / jnp.sqrt(
        samples * (mean_trait[:, None] + EPSILON) * (mean_pred[None, :] + EPSILON)
    )
    return (variant_z, gene_z)


def solution(mesh):
    return jax.shard_map(
        per_device,
        mesh=mesh,
        in_specs=(P("samp", "pos"), P("samp", None), P("pos", None), P(), P()),
        out_specs=(P("samp", "pos"), P("samp", "pos")),
        check_vma=False,
    )
```

time: 339 us -> 184 us (0.54)
  waiting for transfers between devices: 214 us -> 0 us
  Pallas kernels: 0 us -> 175 us
  blocking collectives: 48 us -> 0 us
  matrix products: 35.4 us -> 0 us
  other arithmetic: 25.7 us -> 6.29 us
  between operations: 14.1 us -> 0.66 us
    reduce_scatter x1 -> x0, waiting for transfers between devices: 214 us -> none  [per_device(): lax.psum_scatter(jnp.concatenate([contract(phenotypes, dosages), contract...]
    pallas_call x0 -> x1, Pallas kernels: none -> 175 us  [reduce_all(): pl.pallas_call(functools.partial(kernel, nz, npos, share), out_shape=(jax...]
    psum x1 -> x0, blocking collectives: 48 us -> none  [per_device(): dose_total, pred_total = lax.psum((dose_sq, pred_sq), 'samp')]
    dot_general x3 -> x0, matrix products: 35.4 us -> none  [the longest x2 29 us: contract(): lax.dot_general(left, right, (((0,), (0,)), ((), ())), preferred_element_...]
    concatenate x1 -> x0, other arithmetic: 11.6 us -> none  [per_device(): jnp.concatenate([contract(phenotypes, dosages), contract(phenotypes, pred...]
    reduce_sum x3 -> x0, other arithmetic: 10.4 us -> none  [the longest x1 5.15 us: per_device(): dose_sq = jnp.sum(jnp.square(dosages.astype(jnp.float32)), axis=0)]
  transfers between devices with their start and end apart: 2 -> 0, of which waited for: 1 -> 0; matrix products, arithmetic and copies ran while one was open for 10% -> 0% of each run, Pallas kernels for 0% -> 0%
where the time goes in v1:
time: 184 us; the launch traced here: 183 us
  Pallas kernels  175 us (95%)
  other arithmetic  6.29 us (3%)
    pallas_call x1, Pallas kernels, reduce_all(): pl.pallas_call(functools.partial(kernel, nz, npos, share), out_shape=(jax...  175 us

profile of v1, /device:TPU:0, one launch (start us, length us, event | category | flops | bytes accessed | tf_op | source)
XLA Modules:
  0.0 183.3 jit_solution(18219895015486617897)
XLA Ops:
  0.6 1.6 and_select_fusion.wt
  2.2 174.8 %shard_map.68 = (f32[16,128,128]{2,1,0:T(8,128)}, f32[24,128]{1,0:T(8,128)}, f32[32,128]{1,0:T(8,128)}) custom-call(bf16[2048,2048]{1,0:T(8,128)(2,1)} %dos.1, bf16[2048,2048]{1,0:T(8,128)(2,1)} %ph.1, bf16[16,2048]{1,0:T(8,128)(2,1)} %and_select_fusion.wt), custom_call_target="tpu_custom_call" | custom-call | flops 17179869184 | bytes 16777216 | tf_op jit(solution)/shard_map/pallas_call | solution.py:317
  177.0 0.7 multiply_bitcast_fusion
  177.7 0.8 add_reduce_fusion
  178.5 1.3 bitcast_multiply_fusion.1
  179.9 0.7 add_bitcast_fusion
  180.6 1.6 copy.8
  182.1 1.2 bitcast_multiply_fusion
  (1 shorter events, 0.0 us)

commit v2 on v1

--- a/solution.py
+++ b/solution.py
@@ -13,13 +13,14 @@
 
 
 def kernel(
-    nz, npos, share, dos, ph, wt, out, ex_out, ar_out,
-    part, r1, r2, r3, xt, ex, e1, e2, e3, ar, a1, a2, a3, pp, pr, pf,
+    nz, npos, share, dos_hbm, ph_hbm, wt, out, ex_out, ar_out,
+    dos, ph, part, r1, r2, r3, zpart, z1, z2, z3, xt, ex, e1, e2, e3, ar, a1, a2, a3, pp, pr, pf,
     s_sem, v_sem, s3_sem, v3_sem, es_sem, ev_sem, es3_sem, ev3_sem, ps_sem, pv_sem,
+    dl_sem, pl_sem,
 ):
     samples, variants = dos.shape
     traits = ph.shape[1]
-    chunks, w, block = part.shape[0], part.shape[4], part.shape[5]
+    chunks, w, block = out.shape
     tile = 2 * block
     me = lax.axis_index("samp")
     mp = lax.axis_index("pos")
@@ -38,6 +39,21 @@
     def ppeer(d):
         return lax.rem(mp + d, npos)
 
+    def load_dos(c):
+        cols = slice(c * w, (c + 1) * w)
+        return pltpu.make_async_copy(dos_hbm.at[:, cols], dos.at[:, cols], dl_sem.at[c])
+
+    def load_ph(i):
+        cols = pl.ds(pl.multiple_of(i * tile, tile), tile)
+        return pltpu.make_async_copy(ph_hbm.at[:, cols], ph.at[:, cols], pl_sem.at[i])
+
+    load_dos(2).start()
+    for i in range(2 * nz):
+        load_ph(i).start()
+    for c in range(chunks):
+        if c != 2:
+            load_dos(c).start()
+
     barrier = pltpu.get_barrier_semaphore()
     peers = [xp, yp] + [zdev(d) for d in range(1, nz)]
     peers += [(me, ppeer(d)) for d in range(1, npos)]
@@ -54,11 +70,15 @@
     def order(c):
         return (mx, my, xp, yp) if c % 2 == 0 else (my, mx, yp, xp)
 
-    def compute(c):
+    def compute(c, first=False):
         cols = slice(c * w, (c + 1) * w)
+        if c < 6:
+            load_dos(c).wait()
         xt[...] = dos[:, cols].T
 
         def body(i, carry):
+            if first:
+                load_ph(i).wait()
             res = jnp.dot(
                 xt[...],
                 ph[:, pl.ds(pl.multiple_of(i * tile, tile), tile)],
@@ -67,26 +87,27 @@
             z, y = i // 2, lax.rem(i, 2)
             for x in range(2):
                 val = res[:, x * block : (x + 1) * block]
-                if c % 2 == 0:
-                    part[c, x, y, z] = val
+                a, b = (x, y) if c % 2 == 0 else (y, x)
+                if c < 2:
+                    zpart[c, z, a, b] = val
                 else:
-                    part[c, y, x, z] = val
+                    part[c - 2, a, b, z] = val
             return carry
 
         lax.fori_loop(0, 2 * nz, body, 0)
 
     def copy1(c):
         f, _, dev, _ = order(c)
-        return remote(part.at[c, 1 - f], r1.at[c], s_sem.at[0, c], v_sem.at[0, c], dev)
+        return remote(part.at[c - 2, 1 - f], r1.at[c - 2], s_sem.at[0, c], v_sem.at[0, c], dev)
 
     def copy2(c):
         f, s, _, dev = order(c)
-        return remote(part.at[c, f, 1 - s], r2.at[c], s_sem.at[1, c], v_sem.at[1, c], dev)
+        return remote(part.at[c - 2, f, 1 - s], r2.at[c - 2], s_sem.at[1, c], v_sem.at[1, c], dev)
 
     def copy3(c, d):
         f, s, _, _ = order(c)
         return remote(
-            part.at[c, f, s, zpeer(d)], r3.at[c, d - 1],
+            part.at[c - 2, f, s, zpeer(d)], r3.at[c - 2, d - 1],
             s3_sem.at[c, d - 1], v3_sem.at[c, d - 1], zdev(d),
         )
 
@@ -95,7 +116,7 @@
         k = 1 - s if other else s
 
         def body(z, carry):
-            part[c, f, k, z] = part[c, f, k, z] + r1[c, k, z]
+            part[c - 2, f, k, z] = part[c - 2, f, k, z] + r1[c - 2, k, z]
             return carry
 
         lax.fori_loop(0, nz, body, 0)
@@ -111,7 +132,7 @@
         copy2(c).wait_recv()
 
         def body(z, carry):
-            part[c, f, s, z] = part[c, f, s, z] + r2[c, z]
+            part[c - 2, f, s, z] = part[c - 2, f, s, z] + r2[c - 2, z]
             return carry
 
         lax.fori_loop(0, nz, body, 0)
@@ -120,11 +141,53 @@
 
     def finish(c):
         f, s, _, _ = order(c)
-        total = part[c, f, s, mz]
+        total = part[c - 2, f, s, mz]
         for d in range(1, nz):
             copy3(c, d).wait_recv()
-            total = total + r3[c, d - 1]
+            total = total + r3[c - 2, d - 1]
         out[c] = total
+
+    def zcopy1(c, d):
+        return remote(
+            zpart.at[c, zpeer(d)], z1.at[c, d - 1],
+            s3_sem.at[c, d - 1], v3_sem.at[c, d - 1], zdev(d),
+        )
+
+    def zcopy2(c):
+        f, _, dev, _ = order(c)
+        return remote(
+            zpart.at[c, mz, 1 - f], z2.at[c], s_sem.at[0, c], v_sem.at[0, c], dev
+        )
+
+    def zcopy3(c):
+        f, s, _, dev = order(c)
+        return remote(
+            zpart.at[c, mz, f, 1 - s], z3.at[c], s_sem.at[1, c], v_sem.at[1, c], dev
+        )
+
+    def zstage2(c):
+        f, _, _, _ = order(c)
+        for d in range(1, nz):
+            zcopy1(c, d).wait_recv()
+        for k in range(2):
+            for m in range(2):
+                total = zpart[c, mz, k, m]
+                for d in range(1, nz):
+                    total = total + z1[c, d - 1, k, m]
+                zpart[c, mz, k, m] = total
+        zcopy2(c).start()
+
+    def zstage3(c):
+        f, _, _, _ = order(c)
+        zcopy2(c).wait_recv()
+        for m in range(2):
+            zpart[c, mz, f, m] = zpart[c, mz, f, m] + z2[c, m]
+        zcopy3(c).start()
+
+    def zfinish(c):
+        f, s, _, _ = order(c)
+        zcopy3(c).wait_recv()
+        out[c] = zpart[c, mz, f, s] + z3[c]
 
     def pcopy(d):
         return remote(
@@ -234,18 +297,28 @@
         ex_out[...] = total
         ar_out[...] = sums
 
-    pairs = chunks // 2
-    for t in range(pairs + 3):
+    pairs = chunks // 2 - 1
+    for t in range(max(pairs + 5, 9)):
         if t == 0:
-            compute(0)
-            copy1(0).start()
-            compute(1)
-            copy1(1).start()
+            compute(2, first=True)
+            copy1(2).start()
+            compute(3)
+            copy1(3).start()
+            for c in range(2):
+                compute(c)
+                for d in range(nz - 1, 0, -1):
+                    zcopy1(c, d).start()
         if t + 1 < pairs:
-            for c in (2 * t + 2, 2 * t + 3):
+            for c in (2 * t + 4, 2 * t + 5):
                 compute(c)
                 copy1(c).start()
+        if 0 <= t < pairs:
+            for c in (2 * t + 2, 2 * t + 3):
+                stage2(c)
         if t == 0:
+            for c in range(chunks):
+                if c >= min(6, 2 * pairs + 2):
+                    load_dos(c).wait()
             predict()
         if t == 1:
             small()
@@ -254,17 +327,28 @@
             small2()
         if t == 3:
             small3()
-        if 0 <= t < pairs:
+        if 0 <= t - 1 < pairs:
             for c in (2 * t, 2 * t + 1):
-                stage2(c)
-        if 0 <= t - 1 < pairs:
-            for c in (2 * t - 2, 2 * t - 1):
                 stage3(c)
-        if 0 <= t - 2 < pairs:
-            for c in (2 * t - 4, 2 * t - 3):
+        if t == 4:
+            zstage2(0)
+            zstage2(1)
+        if t == 5:
+            zstage3(0)
+            zstage3(1)
+        if t == 6:
+            small4()
+            zfinish(0)
+            zfinish(1)
+        if 0 <= t - 4 < pairs:
+            for c in (2 * t - 6, 2 * t - 5):
                 finish(c)
-    small4()
-    for c in range(chunks):
+    for c in range(2):
+        zcopy2(c).wait_send()
+        zcopy3(c).wait_send()
+        for d in range(1, nz):
+            zcopy1(c, d).wait_send()
+    for c in range(2, chunks):
         copy1(c).wait_send()
         copy2(c).wait_send()
         for d in range(1, nz):
@@ -291,10 +375,16 @@
     dma = pltpu.SemaphoreType.DMA
     nq = max(npos - 1, 1)
     scratch = [
-        vm((chunks, 2, 2, nz, w, block), f32),
-        vm((chunks, 2, nz, w, block), f32),
-        vm((chunks, nz, w, block), f32),
-        vm((chunks, nz - 1, w, block), f32),
+        vm((samples, variants), jnp.bfloat16),
+        vm((samples, traits), jnp.bfloat16),
+        vm((chunks - 2, 2, 2, nz, w, block), f32),
+        vm((chunks - 2, 2, nz, w, block), f32),
+        vm((chunks - 2, nz, w, block), f32),
+        vm((chunks - 2, nz - 1, w, block), f32),
+        vm((2, nz, 2, 2, w, block), f32),
+        vm((2, nz - 1, 2, 2, w, block), f32),
+        vm((2, 2, w, block), f32),
+        vm((2, w, block), f32),
         vm((w, samples), jnp.bfloat16),
         vm((2, 2, nz, g + 8, block), f32),
         vm((2, nz, g + 8, block), f32),
@@ -312,6 +402,7 @@
         dma((4,)), dma((4,)),
         dma((2, nz - 1)), dma((2, nz - 1)),
         dma((nq,)), dma((nq,)),
+        dma((chunks,)), dma((2 * nz,)),
     ]
     flops = 2 * samples * variants * traits
     return pl.pallas_call(
@@ -321,7 +412,8 @@
             jax.ShapeDtypeStruct((g + 8, block), f32),
             jax.ShapeDtypeStruct((chunks + g, w), f32),
         ),
-        in_specs=[pl.BlockSpec(memory_space=pltpu.VMEM)] * 3,
+        in_specs=[pl.BlockSpec(memory_space=pl.ANY)] * 2
+        + [pl.BlockSpec(memory_space=pltpu.VMEM)],
         out_specs=[pl.BlockSpec(memory_space=pltpu.VMEM)] * 3,
         scratch_shapes=scratch,
         compiler_params=pltpu.CompilerParams(

time: 184 us -> 168 us (0.913)
  Pallas kernels: 175 us -> 159 us
    pallas_call x1, Pallas kernels: 175 us -> 159 us  [reduce_all(): pl.pallas_call(functools.partial(kernel, nz, npos, share), out_shape=(jax...]
where the time goes in v2:
time: 168 us; the launch traced here: 167 us
  Pallas kernels  159 us (95%)
  other arithmetic  6.29 us (4%)
    pallas_call x1, Pallas kernels, reduce_all(): pl.pallas_call(functools.partial(kernel, nz, npos, share), out_shape=(jax...  159 us

profile of v2, /device:TPU:0, one launch (start us, length us, event | category | flops | bytes accessed | tf_op | source)
XLA Modules:
  0.0 167.4 jit_solution(15422657252262669999)
XLA Ops:
  0.6 1.6 and_select_fusion.wt
  2.2 158.9 %shard_map.68 = (f32[16,128,128]{2,1,0:T(8,128)}, f32[24,128]{1,0:T(8,128)}, f32[32,128]{1,0:T(8,128)}) custom-call(bf16[2048,2048]{1,0:T(8,128)(2,1)} %dos_hbm.1, bf16[2048,2048]{1,0:T(8,128)(2,1)} %ph_hbm.1, bf16[16,2048]{1,0:T(8,128)(2,1)} %and_select_fusion.wt), custom_call_target="tpu_custom_call" | custom-call | flops 17179869184 | bytes 16777216 | tf_op jit(solution)/shard_map/pallas_call | solution.py:408
  161.2 0.7 multiply_bitcast_fusion
  161.8 0.8 add_reduce_fusion
  162.6 1.3 bitcast_multiply_fusion.1
  164.0 0.7 add_bitcast_fusion
  164.7 1.6 copy.8
  166.2 1.2 bitcast_multiply_fusion
  (1 shorter events, 0.0 us)

commit v3 on v2

--- a/solution.py
+++ b/solution.py
@@ -72,7 +72,7 @@
 
     def compute(c, first=False):
         cols = slice(c * w, (c + 1) * w)
-        if c < 6:
+        if c < 8:
             load_dos(c).wait()
         xt[...] = dos[:, cols].T
 
@@ -213,13 +213,17 @@
             pcopy(d).start()
 
     def squares(ref, cols, width):
-        step = min(samples, 128)
+        step = min(samples, 256)
 
         def body(i, acc):
             v = ref[pl.ds(pl.multiple_of(i * step, step), step), cols].astype(jnp.float32)
             return acc + jnp.sum(v * v, axis=0, keepdims=True)
 
         return lax.fori_loop(0, samples // step, body, jnp.zeros((1, width), jnp.float32))
+
+    def dose_squares():
+        for c in range(chunks):
+            ar[c : c + 1, :] = squares(dos, slice(c * w, (c + 1) * w), w)
 
     def small():
         pred = pp[mp]
@@ -233,8 +237,6 @@
         ar[chunks : chunks + pf.shape[0], :] = jnp.broadcast_to(
             jnp.sum(full * full, axis=1, keepdims=True), (pf.shape[0], w)
         )
-        for c in range(chunks):
-            ar[c : c + 1, :] = squares(dos, slice(c * w, (c + 1) * w), w)
         g = pf.shape[0]
 
         def body(i, carry):
@@ -308,8 +310,12 @@
                 compute(c)
                 for d in range(nz - 1, 0, -1):
                     zcopy1(c, d).start()
-        if t + 1 < pairs:
-            for c in (2 * t + 4, 2 * t + 5):
+            if pairs > 1:
+                for c in (4, 5):
+                    compute(c)
+                    copy1(c).start()
+        if t + 2 < pairs:
+            for c in (2 * t + 6, 2 * t + 7):
                 compute(c)
                 copy1(c).start()
         if 0 <= t < pairs:
@@ -317,15 +323,17 @@
                 stage2(c)
         if t == 0:
             for c in range(chunks):
-                if c >= min(6, 2 * pairs + 2):
+                if c >= min(8, 2 * pairs + 2):
                     load_dos(c).wait()
             predict()
         if t == 1:
+            dose_squares()
+        if t == 2:
             small()
             small1()
-        if t == 2:
+        if t == 3:
             small2()
-        if t == 3:
+        if t == 4:
             small3()
         if 0 <= t - 1 < pairs:
             for c in (2 * t, 2 * t + 1):

time: 168 us -> 171 us (1.018)
  Pallas kernels: 159 us -> 162 us
    pallas_call x1, Pallas kernels: 159 us -> 162 us  [reduce_all(): pl.pallas_call(functools.partial(kernel, nz, npos, share), out_shape=(jax...]
where the time goes in v3:
time: 171 us; the launch traced here: 170 us
  Pallas kernels  162 us (95%)
  other arithmetic  6.29 us (4%)
    pallas_call x1, Pallas kernels, reduce_all(): pl.pallas_call(functools.partial(kernel, nz, npos, share), out_shape=(jax...  162 us

profile of v3, /device:TPU:0, one launch (start us, length us, event | category | flops | bytes accessed | tf_op | source)
XLA Modules:
  0.0 170.2 jit_solution(12253534238931532313)
XLA Ops:
  0.6 1.6 and_select_fusion.wt
  2.2 161.7 %shard_map.68 = (f32[16,128,128]{2,1,0:T(8,128)}, f32[24,128]{1,0:T(8,128)}, f32[32,128]{1,0:T(8,128)}) custom-call(bf16[2048,2048]{1,0:T(8,128)(2,1)} %dos_hbm.1, bf16[2048,2048]{1,0:T(8,128)(2,1)} %ph_hbm.1, bf16[16,2048]{1,0:T(8,128)(2,1)} %and_select_fusion.wt), custom_call_target="tpu_custom_call" | custom-call | flops 17179869184 | bytes 16777216 | tf_op jit(solution)/shard_map/pallas_call | solution.py:416
  164.0 0.7 multiply_bitcast_fusion
  164.7 0.8 add_reduce_fusion
  165.4 1.3 bitcast_multiply_fusion.1
  166.8 0.7 add_bitcast_fusion
  167.5 1.6 copy.8
  169.1 1.2 bitcast_multiply_fusion
  (1 shorter events, 0.0 us)

commit v4 on v3

--- a/solution.py
+++ b/solution.py
@@ -72,7 +72,7 @@
 
     def compute(c, first=False):
         cols = slice(c * w, (c + 1) * w)
-        if c < 8:
+        if c < 6:
             load_dos(c).wait()
         xt[...] = dos[:, cols].T
 
@@ -310,12 +310,8 @@
                 compute(c)
                 for d in range(nz - 1, 0, -1):
                     zcopy1(c, d).start()
-            if pairs > 1:
-                for c in (4, 5):
-                    compute(c)
-                    copy1(c).start()
-        if t + 2 < pairs:
-            for c in (2 * t + 6, 2 * t + 7):
+        if t + 1 < pairs:
+            for c in (2 * t + 4, 2 * t + 5):
                 compute(c)
                 copy1(c).start()
         if 0 <= t < pairs:
@@ -323,7 +319,7 @@
                 stage2(c)
         if t == 0:
             for c in range(chunks):
-                if c >= min(8, 2 * pairs + 2):
+                if c >= min(6, 2 * pairs + 2):
                     load_dos(c).wait()
             predict()
         if t == 1:
@@ -338,14 +334,15 @@
         if 0 <= t - 1 < pairs:
             for c in (2 * t, 2 * t + 1):
                 stage3(c)
-        if t == 4:
+        if t == pairs:
             zstage2(0)
             zstage2(1)
-        if t == 5:
+        if t == pairs + 1:
             zstage3(0)
             zstage3(1)
         if t == 6:
             small4()
+        if t == pairs + 2:
             zfinish(0)
             zfinish(1)
         if 0 <= t - 4 < pairs:

time: 171 us -> 165 us (0.965)
  Pallas kernels: 162 us -> 156 us
    pallas_call x1, Pallas kernels: 162 us -> 156 us  [reduce_all(): pl.pallas_call(functools.partial(kernel, nz, npos, share), out_shape=(jax...]
where the time goes in v4:
time: 165 us
  Pallas kernels  156 us (95%)
  other arithmetic  6.29 us (4%)
    pallas_call x1, Pallas kernels, reduce_all(): pl.pallas_call(functools.partial(kernel, nz, npos, share), out_shape=(jax...  156 us

profile of v4, /device:TPU:0, one launch (start us, length us, event | category | flops | bytes accessed | tf_op | source)
XLA Modules:
  0.0 164.6 jit_solution(5420874529698772160)
XLA Ops:
  0.6 1.6 and_select_fusion.wt
  2.2 156.1 %shard_map.68 = (f32[16,128,128]{2,1,0:T(8,128)}, f32[24,128]{1,0:T(8,128)}, f32[32,128]{1,0:T(8,128)}) custom-call(bf16[2048,2048]{1,0:T(8,128)(2,1)} %dos_hbm.1, bf16[2048,2048]{1,0:T(8,128)(2,1)} %ph_hbm.1, bf16[16,2048]{1,0:T(8,128)(2,1)} %and_select_fusion.wt), custom_call_target="tpu_custom_call" | custom-call | flops 17179869184 | bytes 16777216 | tf_op jit(solution)/shard_map/pallas_call | solution.py:413
  158.3 0.7 multiply_bitcast_fusion
  159.0 0.8 add_reduce_fusion
  159.8 1.3 bitcast_multiply_fusion.1
  161.2 0.7 add_bitcast_fusion
  161.9 1.6 copy.8
  163.4 1.2 bitcast_multiply_fusion
  (1 shorter events, 0.0 us)

commit v5 on v4

--- a/solution.py
+++ b/solution.py
@@ -20,7 +20,7 @@
 ):
     samples, variants = dos.shape
     traits = ph.shape[1]
-    chunks, w, block = out.shape
+    chunks, w, block = variants // WIDTH, WIDTH, out.shape[0]
     tile = 2 * block
     me = lax.axis_index("samp")
     mp = lax.axis_index("pos")
@@ -145,7 +145,7 @@
         for d in range(1, nz):
             copy3(c, d).wait_recv()
             total = total + r3[c - 2, d - 1]
-        out[c] = total
+        out[:, c * w : (c + 1) * w] = total.T
 
     def zcopy1(c, d):
         return remote(
@@ -187,7 +187,7 @@
     def zfinish(c):
         f, s, _, _ = order(c)
         zcopy3(c).wait_recv()
-        out[c] = zpart[c, mz, f, s] + z3[c]
+        out[:, c * w : (c + 1) * w] = (zpart[c, mz, f, s] + z3[c]).T
 
     def pcopy(d):
         return remote(
@@ -413,7 +413,7 @@
     return pl.pallas_call(
         functools.partial(kernel, nz, npos, share),
         out_shape=(
-            jax.ShapeDtypeStruct((chunks, w, block), f32),
+            jax.ShapeDtypeStruct((block, variants), f32),
             jax.ShapeDtypeStruct((g + 8, block), f32),
             jax.ShapeDtypeStruct((chunks + g, w), f32),
         ),
@@ -442,12 +442,12 @@
     masked_t = jnp.where(inside, weights_t, jnp.zeros_like(weights_t))
     out, extra, sums = reduce_all(dosages, phenotypes, masked_t, n, npos, share)
     samples = dosages.shape[0] * n
-    chunks = out.shape[0]
+    chunks = variants // WIDTH
     g = sums.shape[0] - chunks
     mean_dose = sums[:chunks].reshape(-1) / samples
     mean_pred = sums[chunks : chunks + share, 0] / samples
     mean_trait = extra[g] / samples
-    marginal = out.reshape(variants, -1).T
+    marginal = out
     variant_z = marginal / jnp.sqrt(
         samples * (mean_trait[:, None] + EPSILON) * (mean_dose[None, :] + EPSILON)
     )

time: 165 us -> 165 us (level)
  no operation moved by 1% of the time
where the time goes in v5:
time: 165 us; the launch traced here: 164 us
  Pallas kernels  156 us (95%)
  other arithmetic  7.51 us (5%)
    pallas_call x1, Pallas kernels, reduce_all(): pl.pallas_call(functools.partial(kernel, nz, npos, share), out_shape=(jax...  156 us

profile of v5, /device:TPU:0, one launch (start us, length us, event | category | flops | bytes accessed | tf_op | source)
XLA Modules:
  0.0 164.4 jit_solution(11140272346776658886)
XLA Ops:
  0.6 1.6 and_select_fusion.wt
  2.2 156.2 %shard_map.68 = (f32[128,2048]{1,0:T(8,128)}, f32[24,128]{1,0:T(8,128)}, f32[32,128]{1,0:T(8,128)}) custom-call(bf16[2048,2048]{1,0:T(8,128)(2,1)} %dos_hbm.1, bf16[2048,2048]{1,0:T(8,128)(2,1)} %ph_hbm.1, bf16[16,2048]{1,0:T(8,128)(2,1)} %and_select_fusion.wt), custom_call_target="tpu_custom_call" | custom-call | flops 17179869184 | bytes 16777216 | tf_op jit(solution)/shard_map/pallas_call | solution.py:413
  158.4 0.7 multiply_bitcast_fusion
  159.1 0.8 add_reduce_fusion
  159.9 1.3 bitcast_multiply_fusion
  161.3 0.7 add_bitcast_fusion
  162.0 2.4 %rsqrt_multiply_fusion = f32[128,2048]{1,0:T(8,128)} fusion(f32[128,2048]{1,0:T(8,128)} %get-tuple-element.5, f32[2048]{0:T(1024)S(1)} %add_bitcast_fusion, f32[128]{0:T(128)S(1)} %multiply_bitcast_fusion), kind=kLoop, calls=%fused_computation | loop fusion | flops 524288 | bytes 2105856 | tf_op jit(solution)/shard_map/div | solution.py:451
  (1 shorter events, 0.0 us)
